TPU v7x, 512 devices: a whole 4x8x8 slice. The times are simulated.
512 devices in a mesh: grp: 8 (over y_lo, core), tile: 64 (over y_hi, x, z).
Axes of the slice: x: 4, y: 8 (y_hi: 2, y_lo: 4; y = y_hi * 4 + y_lo), z: 8, core: 2. Of those that a mesh axis runs over, the one named last changes fastest.
Arguments:
- hidden: bfloat16 [8, 512, 128, 128], P('grp', 'tile'), may hold values from -13 to 13
- cotangent: float32 [8, 512, 128], P('grp', 'tile'), may hold values from -16 to 16
- spectral_w: bfloat16 [4096, 256], P('tile'), may hold values from -0.375 to 0.375
- conv_k: float32 [9, 128], replicated, may hold values from -2 to 2
- proj_w: float32 [128], replicated, may hold values from -0.5 to 0.5
Outputs:
- grad_hidden: float32 [8, 512, 128, 128], P('grp', 'tile')
- grad_spectral: float32 [4096, 256], P('tile')
- grad_conv: float32 [9, 128], replicated
- grad_proj: float32 [128], replicated
All inputs are finite; a program needn't handle non-finite values.
Results may differ from a plain program's by a relative error of at most 0.015.
Values may be sent and summed in bfloat16 or wider, within the bound.
No kernel may reach another device: no remote copies, remote signals or barrier semaphores. Data moves between devices by JAX's collectives and lax.ppermute only.
A program may use at most 64 MiB of HBM per device.

v0:
```python
import jax
import jax.numpy as jnp
from jax import lax
from jax.sharding import PartitionSpec as P

HIGH = lax.Precision.HIGHEST


def padded(block, sides, width):
    for axis, dim in sides:
        count = lax.axis_size(axis)
        forward = [(i, i + 1) for i in range(count - 1)]
        backward = [(target, source) for source, target in forward]
        low = lax.ppermute(
            lax.slice_in_dim(block, block.shape[dim] - width, None, axis=dim), axis, forward
        )
        high = lax.ppermute(lax.slice_in_dim(block, 0, width, axis=dim), axis, backward)
        block = jnp.concatenate([low, block, high], axis=dim)
    return block


def spectral_tables(modes, bins):
    mode_idx = jnp.arange(modes, dtype=jnp.int32)
    bin_idx = jnp.arange(bins, dtype=jnp.int32)
    phase_int = mode_idx[:, None] * bin_idx[None, :] % bins
    angle_val = phase_int.astype(jnp.float32) * (2.0 * jnp.pi / bins)
    cosine = jnp.cos(angle_val)
    sine = jnp.sin(angle_val)
    forward_tab = jnp.concatenate([cosine, -sine], 0).astype(jnp.bfloat16)
    weight_k = jnp.where(mode_idx == 0, 1.0, 2.0).astype(jnp.float32)[:, None] / bins
    inverse_tab = jnp.concatenate([cosine * weight_k, -sine * weight_k], 0).T.astype(jnp.bfloat16)
    return (forward_tab, inverse_tab)


def build_mixer(weights, modes, chans):
    real_w = weights[:, :chans].reshape(modes, chans, chans)
    imag_w = weights[:, chans:].reshape(modes, chans, chans)
    upper = jnp.concatenate([real_w, imag_w], 2)
    lower = jnp.concatenate([-imag_w, real_w], 2)
    return jnp.concatenate([upper, lower], 1)


def gelu_pair(value):
    normal_cdf = 0.5 * (1.0 + jax.scipy.special.erf(value * 0.7071067811865476))
    return (
        value * normal_cdf,
        normal_cdf + value * jnp.exp(-0.5 * value * value) * 0.3989422804014327,
    )


def cell_backward(hidden_cells, local_term, cot_cells, mixer, forward_tab, inverse_tab, proj_w):
    modes = mixer.shape[0]
    chans = proj_w.shape[0]
    spec_h = jnp.einsum(
        "jb,pbc->jpc", forward_tab, hidden_cells, preferred_element_type=jnp.float32
    ).astype(jnp.bfloat16)
    h_cat = jnp.concatenate([spec_h[:modes], spec_h[modes:]], 2)
    mixed = jnp.einsum("kpa,kab->kpb", h_cat, mixer, preferred_element_type=jnp.float32).astype(
        jnp.bfloat16
    )
    mixed_stack = jnp.concatenate([mixed[:, :, :chans], mixed[:, :, chans:]], 0)
    spectral_out = jnp.einsum(
        "bj,jpo->pbo", inverse_tab, mixed_stack, preferred_element_type=jnp.float32
    )
    pre_act = spectral_out + local_term
    activ, slope = gelu_pair(pre_act)
    proj_grad = jnp.einsum("pb,pbo->o", cot_cells, activ, precision=HIGH)
    grad_pre = (cot_cells[:, :, None] * proj_w * slope).astype(jnp.bfloat16)
    grad_mix = jnp.einsum(
        "bj,pbo->jpo", inverse_tab, grad_pre, preferred_element_type=jnp.float32
    ).astype(jnp.bfloat16)
    grad_real = grad_mix[:modes]
    grad_imag = grad_mix[modes:]
    grad_cat = jnp.concatenate([grad_real, grad_imag], 2)
    grad_spec = jnp.einsum(
        "kpb,kab->kpa", grad_cat, mixer, preferred_element_type=jnp.float32
    ).astype(jnp.bfloat16)
    grad_stack = jnp.concatenate([grad_spec[:, :, :chans], grad_spec[:, :, chans:]], 0)
    grad_in = jnp.einsum("jb,jpc->pbc", forward_tab, grad_stack, preferred_element_type=jnp.float32)
    left_side = jnp.concatenate([spec_h[:modes], spec_h[modes:]], 1)
    right_side = jnp.concatenate([grad_cat, jnp.concatenate([grad_imag, -grad_real], 2)], 1)
    weight_term = jnp.einsum(
        "kpc,kpo->kco", left_side, right_side, preferred_element_type=jnp.float32
    ).reshape(modes * chans, 2 * chans)
    return (grad_pre, grad_in, weight_term, proj_grad)


def local(hidden, cotangent, spectral_w, conv_k, proj_w):
    rows_here, cols_here, bins_here, chans = hidden.shape
    modes = spectral_w.shape[0] * lax.axis_size("tile") // chans
    cell_count = rows_here * cols_here
    forward_tab, inverse_tab = spectral_tables(modes, bins_here)
    x_pad = padded(hidden, (("grp", 0), ("tile", 1)), 1)
    offsets = [(row_off, col_off) for row_off in (-1, 0, 1) for col_off in (-1, 0, 1)]
    local_term = jnp.zeros((rows_here, cols_here, bins_here, chans), jnp.float32)
    for index_d, (row_off, col_off) in enumerate(offsets):
        window = x_pad[1 + row_off : 1 + row_off + rows_here, 1 + col_off : 1 + col_off + cols_here]
        local_term = local_term + window.astype(jnp.float32) * conv_k[index_d]
    whole_w = lax.all_gather(spectral_w, "tile", axis=0, tiled=True)
    mixer = build_mixer(whole_w, modes, chans)
    grad_pre, grad_in, weight_term, proj_grad = cell_backward(
        hidden.reshape(cell_count, bins_here, chans),
        local_term.reshape(cell_count, bins_here, chans),
        cotangent.reshape(cell_count, bins_here),
        mixer,
        forward_tab,
        inverse_tab,
        proj_w,
    )
    grad_block = grad_pre.reshape(rows_here, cols_here, bins_here, chans)
    conv_part = jnp.stack(
        [
            jnp.einsum(
                "xybc,xybc->c",
                x_pad[1 + row_off : 1 + row_off + rows_here, 1 + col_off : 1 + col_off + cols_here],
                grad_block,
                preferred_element_type=jnp.float32,
            )
            for row_off, col_off in offsets
        ],
        0,
    )
    grad_pad = padded(grad_block, (("grp", 0), ("tile", 1)), 1)
    grad_hidden = grad_in.reshape(rows_here, cols_here, bins_here, chans)
    for index_d, (row_off, col_off) in enumerate(offsets):
        window = grad_pad[
            1 - row_off : 1 - row_off + rows_here, 1 - col_off : 1 - col_off + cols_here
        ]
        grad_hidden = grad_hidden + window.astype(jnp.float32) * conv_k[index_d]
    tile_share = lax.psum_scatter(weight_term, "tile", scatter_dimension=0, tiled=True)
    grad_spectral = lax.psum(tile_share.astype(jnp.bfloat16), "grp").astype(jnp.float32)
    conv_all, proj_all = lax.psum((conv_part, proj_grad), ("grp", "tile"))
    return (grad_hidden, grad_spectral, conv_all, proj_all)


def solution(mesh):
    in_specs = (P("grp", "tile", None, None), P("grp", "tile", None), P("tile", None), P(), P())
    out_specs = (P("grp", "tile", None, None), P("tile", None), P(), P())
    return jax.shard_map(local, mesh=mesh, in_specs=in_specs, out_specs=out_specs, check_vma=False)
```

profile of v0, /device:TPU:1, one launch (start us, length us, event | category | flops | bytes accessed | tf_op | source)
XLA Modules:
  0.0 639.4 jit_solution(11236863667525213482)
XLA Ops:
  7.2 0.0 all-gather.2.cloned.1.call-start
  7.2 0.7 all-gather.2.cloned.1.call-update
  7.9 0.0 reduce-scatter.2.cloned.1.call-start
  7.9 1.1 copy.11
  9.1 8.8 %collective-permute-start.1 = (bf16[1,8,128,128]{2,3,1,0:T(8,128)(2,1)S(1)}, bf16[1,8,128,128]{2,3,1,0:T(8,128)(2,1)S(1)}, u32[]{:S(2)}, u32[]{:S(2)}) collective-permute-start(bf16[1,8,128,128]{2,3,1,0:T(8,128)(2,1)S(1)} %copy.11), channel_id=1, source_target_pairs={{64,0},{128,64},{192,128},{256,192},{320,256},{384,320},{448,384},... | collective-permute-start | bytes 786440 | tf_op jit(solution)/shard_map/ppermute | solution.py:17
  17.9 1.9 collective-permute-start
  19.8 0.1 fusion.41
  19.9 1.1 convolution_convert_fusion.1
  21.1 1.0 slice_bitcast_fusion.8
  22.1 0.0 copy-start.7
  22.1 0.0 copy-start.9
  22.1 0.0 copy-start.11
  22.1 0.0 copy-start.13
  22.1 0.0 copy-start.15
  22.1 0.0 copy-start.17
  22.1 0.0 copy-start.19
  22.2 0.0 copy-start.21
  22.2 0.1 multiply_convert_fusion.1
  22.3 0.0 collective-permute-done.1
  22.3 0.8 collective-permute-done
  23.1 1.3 collective-permute-start.3
  24.4 4.0 collective-permute-start.2
  28.4 119.3 %all-gather.2.cloned.1.call-done = bf16[4096,256]{1,0:T(8,128)(2,1)} async-done(((bf16[64,256]{1,0:T(8,128)(2,1)}), bf16[4096,256]{1,0:T(8,128)(2,1)}) %all-gather.2.cloned.1.call-update) | async-done | bytes 2097168 | tf_op jit(solution)/shard_map/all_gather | solution.py:99
  147.7 1.7 fusion.52
  149.4 0.0 copy-start.2
  149.4 0.3 neg.13
  149.7 0.0 copy-start.1
  149.7 0.0 copy-start.23
  149.7 0.0 copy-start.25
  149.7 0.9 fusion.2
  150.6 0.0 copy-done.2
  150.6 0.2 copy-done.1
  150.8 0.0 collective-permute-done.3
  150.8 0.0 collective-permute-done.2
  150.9 1.6 bitcast_convert_fusion
  152.5 0.2 convolution_convert_fusion
  152.8 0.0 copy-start
  152.8 2.7 fusion.24
  155.5 0.0 reduce-scatter.2.cloned.1.call-update
  155.5 6.4 %collective-permute-start.5 = (bf16[1,8,128,128]{2,3,1,0:T(8,128)(2,1)S(1)}, bf16[1,8,128,128]{2,3,1,0:T(8,128)(2,1)}, u32[]{:S(2)}, u32[]{:S(2)}) collective-permute-start(bf16[1,8,128,128]{2,3,1,0:T(8,128)(2,1)S(1)} %bitcast.128), channel_id=1, source_target_pairs={{64,0},{128,64},{192,128},{256,192},{320,256},{384,320},{448,384},... | collective-permute-start | bytes 786440 | tf_op jit(solution)/shard_map/ppermute | solution.py:17
  161.9 5.1 collective-permute-start.4
  167.0 0.2 copy.51
  167.2 0.2 multiply_reduce_fusion
  167.4 1.0 fusion.14
  168.4 1.2 fusion.15
  169.6 0.0 copy-start.26
  169.6 0.0 copy-start.12
  169.7 3.2 fusion.3
  172.9 0.6 convolution_bitcast_fusion.2
  173.5 97.4 %all-reduce = (f32[9,128]{1,0:T(8,128)}, f32[128]{0:T(128)}) all-reduce(f32[9,128]{1,0:T(8,128)S(1)} %stack.39, f32[128]{0:T(128)S(1)} %convolution_bitcast_fusion.2), channel_id=1, replica_groups=mesh['grp'=8,'tile'=64] {'grp','tile'}, use_global_device_ids=true, to_apply=%region_2.3 | all-reduce | flops 1280 | bytes 10240 | tf_op jit(solution)/shard_map/psum | solution.py:132
  270.9 0.0 collective-permute-done.5
  270.9 0.0 collective-permute-done.4
  270.9 0.8 pad_maximum_fusion.23
  271.8 1.3 collective-permute-start.6
  273.1 4.0 collective-permute-start.7
  277.1 0.4 collective-permute-done.6
  277.5 1.3 collective-permute-done.7
  278.9 0.0 copy-done.10
  278.9 2.1 fusion.21
  281.1 1.0 copy.20
  282.1 273.8 %reduce-scatter.2.cloned.1.call-done = f32[64,256]{1,0:T(8,128)} async-done(((f32[4096,256]{1,0:T(8,128)}), f32[64,256]{1,0:T(8,128)}) %reduce-scatter.2.cloned.1.call-update) | async-done | bytes 65552 | tf_op jit(solution)/shard_map/reduce_scatter | solution.py:130
  555.8 0.8 convert_element_type.112
  556.7 75.3 %psum.21 = bf16[64,256]{1,0:T(8,128)(2,1)S(1)} all-reduce(bf16[64,256]{1,0:T(8,128)(2,1)S(1)} %convert_element_type.112), channel_id=1, replica_groups=mesh['grp'=8,'tile'=64] {'grp'}, use_global_device_ids=true, to_apply=%region_1.2 | all-reduce | flops 16384 | bytes 65536 | tf_op jit(solution)/shard_map/psum | solution.py:131
  632.0 0.6 convert_element_type.113
  (49 shorter events, 0.3 us)
Async XLA Ops:
  7.2 140.5 %all-gather.2.cloned.1.call-start = ((), (), s32[]{:S(2)}) async-start(), calls=%async_computation.1 | async-start | bytes 2129920 | tf_op jit(solution)/shard_map/all_gather | solution.py:99
  7.9 548.0 %reduce-scatter.2.cloned.1.call-start = ((), (), s32[]{:S(2)}) async-start(), calls=%async_computation.2 | async-start | bytes 4259840 | tf_op jit(solution)/shard_map/reduce_scatter | solution.py:130
  9.1 13.2 %collective-permute-start.1 = (bf16[1,8,128,128]{2,3,1,0:T(8,128)(2,1)S(1)}, bf16[1,8,128,128]{2,3,1,0:T(8,128)(2,1)S(1)}, u32[]{:S(2)}, u32[]{:S(2)}) collective-permute-start(bf16[1,8,128,128]{2,3,1,0:T(8,128)(2,1)S(1)} %copy.11), channel_id=1, source_target_pairs={{64,0},{128,64},{192,128},{256,192},{320,256},{384,320},{448,384},... | collective-permute-start | bytes 786440 | tf_op jit(solution)/shard_map/ppermute | solution.py:17
  17.9 5.2 collective-permute-start
  22.1 128.7 %copy-start.5 = (f32[128]{0:T(128)}, f32[128]{0:T(128)S(1)}, u32[]{:S(2)}) copy-start(f32[128]{0:T(128)S(1)} %get-tuple-element.35) | copy-start | bytes 1540
  22.1 128.7 %copy-start.7 = (f32[128]{0:T(128)}, f32[128]{0:T(128)S(1)}, u32[]{:S(2)}) copy-start(f32[128]{0:T(128)S(1)} %get-tuple-element.36) | copy-start | bytes 1540
  22.1 128.7 %copy-start.9 = (f32[128]{0:T(128)}, f32[128]{0:T(128)S(1)}, u32[]{:S(2)}) copy-start(f32[128]{0:T(128)S(1)} %get-tuple-element.37) | copy-start | bytes 1540
  22.1 128.7 %copy-start.11 = (f32[128]{0:T(128)}, f32[128]{0:T(128)S(1)}, u32[]{:S(2)}) copy-start(f32[128]{0:T(128)S(1)} %get-tuple-element.38) | copy-start | bytes 1540
  22.1 128.7 %copy-start.13 = (f32[128]{0:T(128)}, f32[128]{0:T(128)S(1)}, u32[]{:S(2)}) copy-start(f32[128]{0:T(128)S(1)} %get-tuple-element.39) | copy-start | bytes 1540
  22.1 128.7 %copy-start.15 = (f32[128]{0:T(128)}, f32[128]{0:T(128)S(1)}, u32[]{:S(2)}) copy-start(f32[128]{0:T(128)S(1)} %get-tuple-element.40) | copy-start | bytes 1540
  22.1 128.7 %copy-start.17 = (f32[128]{0:T(128)}, f32[128]{0:T(128)S(1)}, u32[]{:S(2)}) copy-start(f32[128]{0:T(128)S(1)} %get-tuple-element.41) | copy-start | bytes 1540
  22.1 128.7 %copy-start.19 = (f32[128]{0:T(128)}, f32[128]{0:T(128)S(1)}, u32[]{:S(2)}) copy-start(f32[128]{0:T(128)S(1)} %get-tuple-element.42) | copy-start | bytes 1540
  22.2 128.7 %copy-start.21 = (f32[128]{0:T(128)}, f32[128]{0:T(128)S(1)}, u32[]{:S(2)}) copy-start(f32[128]{0:T(128)S(1)} %get-tuple-element.43) | copy-start | bytes 1540
  23.1 127.7 %collective-permute-start.3 = (bf16[3,1,128,128]{2,3,1,0:T(8,128)(2,1)S(1)}, bf16[3,1,128,128]{2,3,1,0:T(8,128)(2,1)S(1)}, u32[]{:S(2)}, u32[]{:S(2)}) collective-permute-start(bf16[3,1,128,128]{2,3,1,0:T(8,128)(2,1)S(1)} %get-tuple-element.24), channel_id=1, source_target_pairs={{1,0},{2,1},{3,2},{4,3},{5,4},{6,5},{7,6},{8,7},{9,8},{10,9},{11,1... | collective-permute-start | bytes 294920 | tf_op jit(solution)/shard_map/ppermute | solution.py:17
  24.4 126.4 %collective-permute-start.2 = (bf16[3,1,128,128]{2,3,1,0:T(8,128)(2,1)S(1)}, bf16[3,1,128,128]{2,3,1,0:T(8,128)(2,1)S(1)}, u32[]{:S(2)}, u32[]{:S(2)}) collective-permute-start(bf16[3,1,128,128]{2,3,1,0:T(8,128)(2,1)S(1)} %get-tuple-element.25), channel_id=1, source_target_pairs={{0,1},{1,2},{2,3},{3,4},{4,5},{5,6},{6,7},{7,8},{8,9},{9,10},{10,1... | collective-permute-start | bytes 294920 | tf_op jit(solution)/shard_map/ppermute | solution.py:14
  149.4 1.2 copy-start.2
  149.7 1.1 copy-start.1
  149.7 1.2 copy-start.23
  149.7 1.2 copy-start.25
  150.8 1.7 copy-start.3
  150.8 1.7 copy-start.4
  152.8 14.5 %copy-start = (bf16[1,8,128,128]{3,2,1,0:T(8,128)(2,1)S(1)}, bf16[1,8,128,128]{3,2,1,0:T(8,128)(2,1)}, u32[]{:S(2)}) copy-start(bf16[1,8,128,128]{3,2,1,0:T(8,128)(2,1)} %param.5) | copy-start | bytes 786436
  155.5 115.4 %collective-permute-start.5 = (bf16[1,8,128,128]{2,3,1,0:T(8,128)(2,1)S(1)}, bf16[1,8,128,128]{2,3,1,0:T(8,128)(2,1)}, u32[]{:S(2)}, u32[]{:S(2)}) collective-permute-start(bf16[1,8,128,128]{2,3,1,0:T(8,128)(2,1)S(1)} %bitcast.128), channel_id=1, source_target_pairs={{64,0},{128,64},{192,128},{256,192},{320,256},{384,320},{448,384},... | collective-permute-start | bytes 786440 | tf_op jit(solution)/shard_map/ppermute | solution.py:17
  161.9 109.0 %collective-permute-start.4 = (bf16[1,8,128,128]{2,3,1,0:T(8,128)(2,1)S(1)}, bf16[1,8,128,128]{2,3,1,0:T(8,128)(2,1)}, u32[]{:S(2)}, u32[]{:S(2)}) collective-permute-start(bf16[1,8,128,128]{2,3,1,0:T(8,128)(2,1)S(1)} %bitcast.129), channel_id=1, source_target_pairs={{0,64},{64,128},{128,192},{192,256},{256,320},{320,384},{384,448},... | collective-permute-start | bytes 786440 | tf_op jit(solution)/shard_map/ppermute | solution.py:14
  169.6 3.3 copy-start.24
  169.6 3.3 copy-start.26
  169.6 109.2 %copy-start.6 = (f32[128]{0:T(128)S(1)}, f32[128]{0:T(128)}, u32[]{:S(2)}) copy-start(f32[128]{0:T(128)} %copy-done.5) | copy-start | bytes 1540
  169.6 109.2 %copy-start.8 = (f32[128]{0:T(128)S(1)}, f32[128]{0:T(128)}, u32[]{:S(2)}) copy-start(f32[128]{0:T(128)} %copy-done.7) | copy-start | bytes 1540
  169.6 109.2 %copy-start.10 = (f32[128]{0:T(128)S(1)}, f32[128]{0:T(128)}, u32[]{:S(2)}) copy-start(f32[128]{0:T(128)} %copy-done.9) | copy-start | bytes 1540
  169.6 109.2 %copy-start.12 = (f32[128]{0:T(128)S(1)}, f32[128]{0:T(128)}, u32[]{:S(2)}) copy-start(f32[128]{0:T(128)} %copy-done.11) | copy-start | bytes 1540
  169.7 109.2 %copy-start.14 = (f32[128]{0:T(128)S(1)}, f32[128]{0:T(128)}, u32[]{:S(2)}) copy-start(f32[128]{0:T(128)} %copy-done.13) | copy-start | bytes 1540
  169.7 109.2 %copy-start.16 = (f32[128]{0:T(128)S(1)}, f32[128]{0:T(128)}, u32[]{:S(2)}) copy-start(f32[128]{0:T(128)} %copy-done.15) | copy-start | bytes 1540
  169.7 109.2 %copy-start.18 = (f32[128]{0:T(128)S(1)}, f32[128]{0:T(128)}, u32[]{:S(2)}) copy-start(f32[128]{0:T(128)} %copy-done.17) | copy-start | bytes 1540
  169.7 109.2 %copy-start.20 = (f32[128]{0:T(128)S(1)}, f32[128]{0:T(128)}, u32[]{:S(2)}) copy-start(f32[128]{0:T(128)} %copy-done.19) | copy-start | bytes 1540
  169.7 109.2 %copy-start.22 = (f32[128]{0:T(128)S(1)}, f32[128]{0:T(128)}, u32[]{:S(2)}) copy-start(f32[128]{0:T(128)} %copy-done.21) | copy-start | bytes 1540
  271.8 5.8 collective-permute-start.6
  273.1 5.8 collective-permute-start.7
Sparse Core Ops, SparseCore 0:
  12.6 135.0 all-gather.1
  155.6 400.1 reduce-scatter.1
where the time goes:
time: 640 us; the launch traced here: 639 us
  waiting for transfers between devices  396 us (62%)
  blocking collectives  173 us (27%)
  starting transfers between devices  32.8 us (5%)
  between operations  14.6 us (2%)
  matrix products  12.4 us (2%)
    reduce_scatter x1, waiting for transfers between devices, local(): lax.psum_scatter(weight_term, 'tile', scatter_dimension=0, tiled=True)  274 us
    all_gather x1, waiting for transfers between devices, local(): whole_w = lax.all_gather(spectral_w, 'tile', axis=0, tiled=True)  119 us
    psum x1, blocking collectives, local(): conv_all, proj_all = lax.psum((conv_part, proj_grad), ('grp', 'tile'))  97.4 us
    psum x1, blocking collectives, local(): lax.psum(tile_share.astype(jnp.bfloat16), 'grp').astype(jnp.float32)  75.3 us
    ppermute x4, starting transfers between devices, padded(): lax.ppermute(lax.slice_in_dim(block, 0, width, axis=dim), axis, backward)  17.8 us
    ppermute x4, starting transfers between devices, padded(): lax.ppermute(lax.slice_in_dim(block, block.shape[dim] - width, None, axis...  15 us
  transfers between devices with their start and end apart: 10, of which 5 were waited for; matrix products, arithmetic and copies ran while one was open for 3% of the time, Pallas kernels for 0%

commit v1 on v0

--- a/solution.py
+++ b/solution.py
@@ -128,7 +128,9 @@
         ]
         grad_hidden = grad_hidden + window.astype(jnp.float32) * conv_k[index_d]
     tile_share = lax.psum_scatter(weight_term, "tile", scatter_dimension=0, tiled=True)
-    grad_spectral = lax.psum(tile_share.astype(jnp.bfloat16), "grp").astype(jnp.float32)
+    grad_spectral = jnp.sum(lax.all_gather(tile_share.astype(jnp.bfloat16), "grp"), axis=0).astype(
+        jnp.float32
+    )
     conv_all, proj_all = lax.psum((conv_part, proj_grad), ("grp", "tile"))
     return (grad_hidden, grad_spectral, conv_all, proj_all)
 

time: 640 us -> 632 us (0.988)
  blocking collectives: 173 us -> 165 us
    psum x1 -> x0, blocking collectives: 75.3 us -> none  [local(): lax.psum(tile_share.astype(jnp.bfloat16), 'grp').astype(jnp.float32)]
    all_gather x0 -> x1, blocking collectives: none -> 67.4 us  [local(): lax.all_gather(tile_share.astype(jnp.bfloat16), 'grp')]
where the time goes in v1:
time: 632 us
  waiting for transfers between devices  396 us (63%)
  blocking collectives  165 us (26%)
  starting transfers between devices  32.8 us (5%)
  between operations  14.6 us (2%)
  matrix products  12.4 us (2%)
    reduce_scatter x1, waiting for transfers between devices, local(): lax.psum_scatter(weight_term, 'tile', scatter_dimension=0, tiled=True)  274 us
    all_gather x1, waiting for transfers between devices, local(): whole_w = lax.all_gather(spectral_w, 'tile', axis=0, tiled=True)  119 us
    psum x1, blocking collectives, local(): conv_all, proj_all = lax.psum((conv_part, proj_grad), ('grp', 'tile'))  97.4 us
    all_gather x1, blocking collectives, local(): lax.all_gather(tile_share.astype(jnp.bfloat16), 'grp')  67.4 us
    ppermute x4, starting transfers between devices, padded(): lax.ppermute(lax.slice_in_dim(block, 0, width, axis=dim), axis, backward)  17.8 us
    ppermute x4, starting transfers between devices, padded(): lax.ppermute(lax.slice_in_dim(block, block.shape[dim] - width, None, axis...  15 us
  transfers between devices with their start and end apart: 10, of which 5 were waited for; matrix products, arithmetic and copies ran while one was open for 3% of the time, Pallas kernels for 0%

profile of v1, /device:TPU:1, one launch (start us, length us, event | category | flops | bytes accessed | tf_op | source)
XLA Modules:
  0.0 631.7 jit_solution(8318704303405119855)
XLA Ops:
  7.2 0.0 all-gather.3.cloned.1.call-start
  7.2 0.7 all-gather.3.cloned.1.call-update
  7.9 0.0 reduce-scatter.2.cloned.1.call-start
  7.9 1.1 copy.11
  9.1 8.8 %collective-permute-start.1 = (bf16[1,8,128,128]{2,3,1,0:T(8,128)(2,1)S(1)}, bf16[1,8,128,128]{2,3,1,0:T(8,128)(2,1)S(1)}, u32[]{:S(2)}, u32[]{:S(2)}) collective-permute-start(bf16[1,8,128,128]{2,3,1,0:T(8,128)(2,1)S(1)} %copy.11), channel_id=1, source_target_pairs={{64,0},{128,64},{192,128},{256,192},{320,256},{384,320},{448,384},... | collective-permute-start | bytes 786440 | tf_op jit(solution)/shard_map/ppermute | solution.py:17
  17.9 1.9 collective-permute-start
  19.8 0.1 fusion.41
  19.9 1.1 convolution_convert_fusion.1
  21.1 1.0 slice_bitcast_fusion.8
  22.1 0.0 copy-start.7
  22.1 0.0 copy-start.9
  22.1 0.0 copy-start.11
  22.1 0.0 copy-start.13
  22.1 0.0 copy-start.15
  22.1 0.0 copy-start.17
  22.1 0.0 copy-start.19
  22.2 0.0 copy-start.21
  22.2 0.1 multiply_convert_fusion.1
  22.3 0.0 collective-permute-done.1
  22.3 0.8 collective-permute-done
  23.1 1.3 collective-permute-start.3
  24.4 4.0 collective-permute-start.2
  28.4 119.3 %all-gather.3.cloned.1.call-done = bf16[4096,256]{1,0:T(8,128)(2,1)} async-done(((bf16[64,256]{1,0:T(8,128)(2,1)}), bf16[4096,256]{1,0:T(8,128)(2,1)}) %all-gather.3.cloned.1.call-update) | async-done | bytes 2097168 | tf_op jit(solution)/shard_map/all_gather | solution.py:99
  147.7 1.7 fusion.52
  149.4 0.0 copy-start.2
  149.4 0.3 neg.13
  149.7 0.0 copy-start.1
  149.7 0.0 copy-start.23
  149.7 0.0 copy-start.25
  149.7 0.9 fusion.2
  150.6 0.0 copy-done.2
  150.6 0.2 copy-done.1
  150.8 0.0 collective-permute-done.3
  150.8 0.0 collective-permute-done.2
  150.9 1.6 bitcast_convert_fusion
  152.5 0.2 convolution_convert_fusion
  152.8 0.0 copy-start
  152.8 2.7 fusion.24
  155.5 0.0 reduce-scatter.2.cloned.1.call-update
  155.5 6.4 %collective-permute-start.5 = (bf16[1,8,128,128]{2,3,1,0:T(8,128)(2,1)S(1)}, bf16[1,8,128,128]{2,3,1,0:T(8,128)(2,1)}, u32[]{:S(2)}, u32[]{:S(2)}) collective-permute-start(bf16[1,8,128,128]{2,3,1,0:T(8,128)(2,1)S(1)} %bitcast.129), channel_id=1, source_target_pairs={{64,0},{128,64},{192,128},{256,192},{320,256},{384,320},{448,384},... | collective-permute-start | bytes 786440 | tf_op jit(solution)/shard_map/ppermute | solution.py:17
  161.9 5.1 collective-permute-start.4
  167.0 0.2 copy.51
  167.2 0.2 multiply_reduce_fusion
  167.4 1.0 fusion.14
  168.4 1.2 fusion.15
  169.6 0.0 copy-start.26
  169.6 0.0 copy-start.12
  169.7 3.2 fusion.3
  172.9 0.6 convolution_bitcast_fusion.2
  173.5 97.4 %all-reduce = (f32[9,128]{1,0:T(8,128)}, f32[128]{0:T(128)}) all-reduce(f32[9,128]{1,0:T(8,128)S(1)} %stack.39, f32[128]{0:T(128)S(1)} %convolution_bitcast_fusion.2), channel_id=1, replica_groups=mesh['grp'=8,'tile'=64] {'grp','tile'}, use_global_device_ids=true, to_apply=%region_2.3 | all-reduce | flops 1280 | bytes 10240 | tf_op jit(solution)/shard_map/psum | solution.py:134
  270.9 0.0 collective-permute-done.5
  270.9 0.0 collective-permute-done.4
  270.9 0.8 pad_maximum_fusion.23
  271.8 1.3 collective-permute-start.6
  273.1 4.0 collective-permute-start.7
  277.1 0.4 collective-permute-done.6
  277.5 1.3 collective-permute-done.7
  278.9 0.0 copy-done.10
  278.9 2.1 fusion.21
  281.1 1.0 copy.20
  282.1 273.8 %reduce-scatter.2.cloned.1.call-done = f32[64,256]{1,0:T(8,128)} async-done(((f32[4096,256]{1,0:T(8,128)}), f32[64,256]{1,0:T(8,128)}) %reduce-scatter.2.cloned.1.call-update) | async-done | bytes 65552 | tf_op jit(solution)/shard_map/reduce_scatter | solution.py:130
  555.8 0.8 convert_element_type.114
  556.7 67.4 %all-gather = bf16[512,256]{1,0:T(8,128)(2,1)S(1)} all-gather(bf16[64,256]{1,0:T(8,128)(2,1)S(1)} %convert_element_type.114), channel_id=2, replica_groups=mesh['grp'=8,'tile'=64] {'grp'}, dimensions={0}, use_global_device_ids=true | all-gather | bytes 294912 | tf_op jit(solution)/shard_map/all_gather | solution.py:131
  624.2 0.6 convert_element_type.115
  (50 shorter events, 0.3 us)
Async XLA Ops:
  7.2 140.5 %all-gather.3.cloned.1.call-start = ((), (), s32[]{:S(2)}) async-start(), calls=%async_computation.1 | async-start | bytes 2129920 | tf_op jit(solution)/shard_map/all_gather | solution.py:99
  7.9 548.0 %reduce-scatter.2.cloned.1.call-start = ((), (), s32[]{:S(2)}) async-start(), calls=%async_computation.2 | async-start | bytes 4259840 | tf_op jit(solution)/shard_map/reduce_scatter | solution.py:130
  9.1 13.2 %collective-permute-start.1 = (bf16[1,8,128,128]{2,3,1,0:T(8,128)(2,1)S(1)}, bf16[1,8,128,128]{2,3,1,0:T(8,128)(2,1)S(1)}, u32[]{:S(2)}, u32[]{:S(2)}) collective-permute-start(bf16[1,8,128,128]{2,3,1,0:T(8,128)(2,1)S(1)} %copy.11), channel_id=1, source_target_pairs={{64,0},{128,64},{192,128},{256,192},{320,256},{384,320},{448,384},... | collective-permute-start | bytes 786440 | tf_op jit(solution)/shard_map/ppermute | solution.py:17
  17.9 5.2 collective-permute-start
  22.1 128.7 %copy-start.5 = (f32[128]{0:T(128)}, f32[128]{0:T(128)S(1)}, u32[]{:S(2)}) copy-start(f32[128]{0:T(128)S(1)} %get-tuple-element.35) | copy-start | bytes 1540
  22.1 128.7 %copy-start.7 = (f32[128]{0:T(128)}, f32[128]{0:T(128)S(1)}, u32[]{:S(2)}) copy-start(f32[128]{0:T(128)S(1)} %get-tuple-element.36) | copy-start | bytes 1540
  22.1 128.7 %copy-start.9 = (f32[128]{0:T(128)}, f32[128]{0:T(128)S(1)}, u32[]{:S(2)}) copy-start(f32[128]{0:T(128)S(1)} %get-tuple-element.37) | copy-start | bytes 1540
  22.1 128.7 %copy-start.11 = (f32[128]{0:T(128)}, f32[128]{0:T(128)S(1)}, u32[]{:S(2)}) copy-start(f32[128]{0:T(128)S(1)} %get-tuple-element.38) | copy-start | bytes 1540
  22.1 128.7 %copy-start.13 = (f32[128]{0:T(128)}, f32[128]{0:T(128)S(1)}, u32[]{:S(2)}) copy-start(f32[128]{0:T(128)S(1)} %get-tuple-element.39) | copy-start | bytes 1540
  22.1 128.7 %copy-start.15 = (f32[128]{0:T(128)}, f32[128]{0:T(128)S(1)}, u32[]{:S(2)}) copy-start(f32[128]{0:T(128)S(1)} %get-tuple-element.40) | copy-start | bytes 1540
  22.1 128.7 %copy-start.17 = (f32[128]{0:T(128)}, f32[128]{0:T(128)S(1)}, u32[]{:S(2)}) copy-start(f32[128]{0:T(128)S(1)} %get-tuple-element.41) | copy-start | bytes 1540
  22.1 128.7 %copy-start.19 = (f32[128]{0:T(128)}, f32[128]{0:T(128)S(1)}, u32[]{:S(2)}) copy-start(f32[128]{0:T(128)S(1)} %get-tuple-element.42) | copy-start | bytes 1540
  22.2 128.7 %copy-start.21 = (f32[128]{0:T(128)}, f32[128]{0:T(128)S(1)}, u32[]{:S(2)}) copy-start(f32[128]{0:T(128)S(1)} %get-tuple-element.43) | copy-start | bytes 1540
  23.1 127.7 %collective-permute-start.3 = (bf16[3,1,128,128]{2,3,1,0:T(8,128)(2,1)S(1)}, bf16[3,1,128,128]{2,3,1,0:T(8,128)(2,1)S(1)}, u32[]{:S(2)}, u32[]{:S(2)}) collective-permute-start(bf16[3,1,128,128]{2,3,1,0:T(8,128)(2,1)S(1)} %get-tuple-element.24), channel_id=1, source_target_pairs={{1,0},{2,1},{3,2},{4,3},{5,4},{6,5},{7,6},{8,7},{9,8},{10,9},{11,1... | collective-permute-start | bytes 294920 | tf_op jit(solution)/shard_map/ppermute | solution.py:17
  24.4 126.4 %collective-permute-start.2 = (bf16[3,1,128,128]{2,3,1,0:T(8,128)(2,1)S(1)}, bf16[3,1,128,128]{2,3,1,0:T(8,128)(2,1)S(1)}, u32[]{:S(2)}, u32[]{:S(2)}) collective-permute-start(bf16[3,1,128,128]{2,3,1,0:T(8,128)(2,1)S(1)} %get-tuple-element.25), channel_id=1, source_target_pairs={{0,1},{1,2},{2,3},{3,4},{4,5},{5,6},{6,7},{7,8},{8,9},{9,10},{10,1... | collective-permute-start | bytes 294920 | tf_op jit(solution)/shard_map/ppermute | solution.py:14
  149.4 1.2 copy-start.2
  149.7 1.1 copy-start.1
  149.7 1.2 copy-start.23
  149.7 1.2 copy-start.25
  150.8 1.7 copy-start.3
  150.8 1.7 copy-start.4
  152.8 14.5 %copy-start = (bf16[1,8,128,128]{3,2,1,0:T(8,128)(2,1)S(1)}, bf16[1,8,128,128]{3,2,1,0:T(8,128)(2,1)}, u32[]{:S(2)}) copy-start(bf16[1,8,128,128]{3,2,1,0:T(8,128)(2,1)} %param.5) | copy-start | bytes 786436
  155.5 115.4 %collective-permute-start.5 = (bf16[1,8,128,128]{2,3,1,0:T(8,128)(2,1)S(1)}, bf16[1,8,128,128]{2,3,1,0:T(8,128)(2,1)}, u32[]{:S(2)}, u32[]{:S(2)}) collective-permute-start(bf16[1,8,128,128]{2,3,1,0:T(8,128)(2,1)S(1)} %bitcast.129), channel_id=1, source_target_pairs={{64,0},{128,64},{192,128},{256,192},{320,256},{384,320},{448,384},... | collective-permute-start | bytes 786440 | tf_op jit(solution)/shard_map/ppermute | solution.py:17
  161.9 109.0 %collective-permute-start.4 = (bf16[1,8,128,128]{2,3,1,0:T(8,128)(2,1)S(1)}, bf16[1,8,128,128]{2,3,1,0:T(8,128)(2,1)}, u32[]{:S(2)}, u32[]{:S(2)}) collective-permute-start(bf16[1,8,128,128]{2,3,1,0:T(8,128)(2,1)S(1)} %bitcast.130), channel_id=1, source_target_pairs={{0,64},{64,128},{128,192},{192,256},{256,320},{320,384},{384,448},... | collective-permute-start | bytes 786440 | tf_op jit(solution)/shard_map/ppermute | solution.py:14
  169.6 3.3 copy-start.24
  169.6 3.3 copy-start.26
  169.6 109.2 %copy-start.6 = (f32[128]{0:T(128)S(1)}, f32[128]{0:T(128)}, u32[]{:S(2)}) copy-start(f32[128]{0:T(128)} %copy-done.5) | copy-start | bytes 1540
  169.6 109.2 %copy-start.8 = (f32[128]{0:T(128)S(1)}, f32[128]{0:T(128)}, u32[]{:S(2)}) copy-start(f32[128]{0:T(128)} %copy-done.7) | copy-start | bytes 1540
  169.6 109.2 %copy-start.10 = (f32[128]{0:T(128)S(1)}, f32[128]{0:T(128)}, u32[]{:S(2)}) copy-start(f32[128]{0:T(128)} %copy-done.9) | copy-start | bytes 1540
  169.6 109.2 %copy-start.12 = (f32[128]{0:T(128)S(1)}, f32[128]{0:T(128)}, u32[]{:S(2)}) copy-start(f32[128]{0:T(128)} %copy-done.11) | copy-start | bytes 1540
  169.7 109.2 %copy-start.14 = (f32[128]{0:T(128)S(1)}, f32[128]{0:T(128)}, u32[]{:S(2)}) copy-start(f32[128]{0:T(128)} %copy-done.13) | copy-start | bytes 1540
  169.7 109.2 %copy-start.16 = (f32[128]{0:T(128)S(1)}, f32[128]{0:T(128)}, u32[]{:S(2)}) copy-start(f32[128]{0:T(128)} %copy-done.15) | copy-start | bytes 1540
  169.7 109.2 %copy-start.18 = (f32[128]{0:T(128)S(1)}, f32[128]{0:T(128)}, u32[]{:S(2)}) copy-start(f32[128]{0:T(128)} %copy-done.17) | copy-start | bytes 1540
  169.7 109.2 %copy-start.20 = (f32[128]{0:T(128)S(1)}, f32[128]{0:T(128)}, u32[]{:S(2)}) copy-start(f32[128]{0:T(128)} %copy-done.19) | copy-start | bytes 1540
  169.7 109.2 %copy-start.22 = (f32[128]{0:T(128)S(1)}, f32[128]{0:T(128)}, u32[]{:S(2)}) copy-start(f32[128]{0:T(128)} %copy-done.21) | copy-start | bytes 1540
  271.8 5.8 collective-permute-start.6
  273.1 5.8 collective-permute-start.7
Sparse Core Ops, SparseCore 0:
  12.6 135.0 all-gather.2
  155.6 400.1 reduce-scatter.1
